TPU v7x, 32 devices: a whole 2x2x4 slice. The times are simulated.
32 devices in a mesh: seq: 8 (over z, x), seg: 4 (over y, core).
Axes of the slice: x: 2, y: 2, z: 4, core: 2. Of those that a mesh axis runs over, the one named last changes fastest.
Arguments:
- tokens: bfloat16 [4, 2048, 1024], P('seg', 'seq'), may hold values from -6 to 6
- article_lengths: int32 [4, 8], P('seg'), may hold values from 1 to 2041, as said below
- gain_one: float32 [1024], replicated, may hold values from 0.1 to 1.9
- bias_one: float32 [1024], replicated, may hold values from -3 to 3
- w_qkv: bfloat16 [1024, 3072], P('seg'), may hold values from -0.25 to 0.25
- w_out: bfloat16 [1024, 1024], P('seg'), may hold values from -0.5 to 0.5
- gain_two: float32 [1024], replicated, may hold values from 0.1 to 1.9
- bias_two: float32 [1024], replicated, may hold values from -3 to 3
- w_up: bfloat16 [1024, 4096], P('seg'), may hold values from -0.1875 to 0.1875
- w_down: bfloat16 [4096, 1024], P('seg'), may hold values from -0.125 to 0.125
- cotangent: bfloat16 [4, 2048, 1024], P('seg', 'seq'), may hold values from -6 to 6
Outputs:
- result: bfloat16 [4, 2048, 1024], P('seg', 'seq')
- input_grad: float32 [4, 2048, 1024], P('seg', 'seq')
- grad_gain_one: float32 [1024], replicated
- grad_bias_one: float32 [1024], replicated
- grad_qkv: float32 [1024, 3072], P('seg', 'seq')
- grad_out: float32 [1024, 1024], P('seg', 'seq')
- grad_gain_two: float32 [1024], replicated
- grad_bias_two: float32 [1024], replicated
- grad_up: float32 [1024, 4096], P('seg', 'seq')
- grad_down: float32 [4096, 1024], P('seg', 'seq')
Inputs may be any that keep to these rules, and one draw needn't show every extreme that they name: `article_lengths`: each row holds 8 article lengths that sum to 2048; one of them, at a place drawn from the seed, exceeds 2048 - 256, the others are at most 32.
All inputs are finite; a program needn't handle non-finite values.
Results may differ from a plain program's by a relative error of at most 0.02.
Values may be sent and summed in bfloat16 or wider, within the bound.
A program may use at most 192 MiB of HBM per device.

v0:
```python
import math

import jax
import jax.numpy as jnp
from jax import lax
from jax.experimental import pallas as pl
from jax.experimental.pallas import tpu as pltpu
from jax.sharding import PartitionSpec as P

HEADS = 8
HEAD_DIM = 128


def passed_along(block, axis, distance):
    devices = range(lax.axis_size(axis))
    route = [(i - distance, i) for i in devices if i - distance in devices]
    return lax.ppermute(block, axis, route)


def shifted(value, axis, by):
    size = lax.axis_size(axis)
    return lax.ppermute(value, axis, [(i, (i + by) % size) for i in range(size)])


def layer_norm(values, gain, bias):
    center = values - jnp.mean(values, axis=-1, keepdims=True)
    spread = jnp.mean(center * center, axis=-1, keepdims=True)
    return center * lax.rsqrt(spread + 1e-05) * gain + bias


def smooth_act(values):
    return jax.nn.gelu(values, approximate=True)


def article_numbers(lengths_row, positions):
    bounds = jnp.cumsum(lengths_row)
    return jnp.sum((positions[:, None] >= bounds[None, :]).astype(jnp.int32), axis=1)


def per_device(
    tokens,
    article_lengths,
    gain_one,
    bias_one,
    w_qkv,
    w_out,
    gain_two,
    bias_two,
    w_up,
    w_down,
    cotangent,
):
    tok_rows = tokens.shape[1]
    model_width = tokens.shape[2]
    head_count = HEADS
    head_size = HEAD_DIM
    scale = 1.0 / math.sqrt(head_size)
    blocks_seq = lax.axis_size("seq")
    my_place = lax.axis_index("seq")
    full_qkv, full_out, full_up, full_down = (
        lax.all_gather(w_qkv, "seg", axis=0, tiled=True),
        lax.all_gather(w_out, "seg", axis=0, tiled=True),
        lax.all_gather(w_up, "seg", axis=0, tiled=True),
        lax.all_gather(w_down, "seg", axis=0, tiled=True),
    )
    inputs = tokens[0].astype(jnp.float32)
    normed, norm_one_back = jax.vjp(layer_norm, inputs, gain_one, bias_one)
    normed_low = normed.astype(jnp.bfloat16)
    projected = jnp.dot(normed_low, full_qkv, preferred_element_type=jnp.float32).astype(
        jnp.bfloat16
    )
    query_low = projected[:, :model_width]
    key_low = projected[:, model_width : 2 * model_width]
    value_low = projected[:, 2 * model_width :]
    query_heads = query_low.reshape(tok_rows, head_count, head_size)
    lengths_row = article_lengths[0]
    positions = my_place * tok_rows + jnp.arange(tok_rows, dtype=jnp.int32)
    query_art = article_numbers(lengths_row, positions)

    def scores_of(key_block, source):
        key_pos = source * tok_rows + jnp.arange(tok_rows, dtype=jnp.int32)
        key_art = article_numbers(lengths_row, key_pos)
        allowed = (key_pos[None, :] <= positions[:, None]) & (
            key_art[None, :] == query_art[:, None]
        )
        raw = (
            jnp.einsum(
                "qhd,khd->hqk",
                query_heads,
                key_block.reshape(tok_rows, head_count, head_size),
                preferred_element_type=jnp.float32,
            )
            * scale
        )
        return jnp.where(allowed[None], raw, -1e30)

    def forward_block(state, key_block, value_block, source):

        def forward_work(operands):
            (top, total, accum), key_now, value_now = operands
            scores = scores_of(key_now, source)
            new_top = jnp.maximum(top, jnp.max(scores, axis=2))
            factor = jnp.exp(top - new_top)
            weights = jnp.exp(scores - new_top[:, :, None])
            total = total * factor + jnp.sum(weights, axis=2)
            gathered = jnp.einsum(
                "hqk,khd->qhd",
                weights.astype(jnp.bfloat16),
                value_now.reshape(tok_rows, head_count, head_size),
                preferred_element_type=jnp.float32,
            ).reshape(tok_rows, model_width)
            accum = accum * jnp.repeat(factor.T, head_size, axis=1) + gathered
            return (new_top, total, accum)

        def forward_keep(operands):
            return operands[0]

        return lax.cond(
            source <= my_place, forward_work, forward_keep, (state, key_block, value_block)
        )

    start_state = (
        jnp.full((head_count, tok_rows), -1e30, jnp.float32),
        jnp.zeros((head_count, tok_rows), jnp.float32),
        jnp.zeros((tok_rows, model_width), jnp.float32),
    )
    state = forward_block(start_state, key_low, value_low, my_place)

    def forward_step(step, carry):
        key_block, value_block, state_now = carry
        key_block, value_block = passed_along((key_block, value_block), "seq", 1)
        source = (my_place - step) % blocks_seq
        return (key_block, value_block, forward_block(state_now, key_block, value_block, source))

    _, _, state = lax.fori_loop(1, blocks_seq, forward_step, (key_low, value_low, state))
    top, total, accum = state
    log_total = top + jnp.log(total)
    attended = accum / jnp.repeat(total.T, head_size, axis=1)
    attended_low = attended.astype(jnp.bfloat16)
    middle = inputs + jnp.dot(attended_low, full_out, preferred_element_type=jnp.float32)
    normed_two, norm_two_back = jax.vjp(layer_norm, middle, gain_two, bias_two)
    normed_two_low = normed_two.astype(jnp.bfloat16)
    hidden = jnp.dot(normed_two_low, full_up, preferred_element_type=jnp.float32)
    activated, act_back = jax.vjp(smooth_act, hidden)
    activated_low = activated.astype(jnp.bfloat16)
    outputs = middle + jnp.dot(activated_low, full_down, preferred_element_type=jnp.float32)
    result = outputs.astype(jnp.bfloat16)[None]
    grad_top = cotangent[0].astype(jnp.float32)
    grad_top_low = cotangent[0]
    grad_down = jnp.einsum(
        "tf,td->fd", activated_low, grad_top_low, preferred_element_type=jnp.float32
    )
    grad_act = jnp.einsum("td,fd->tf", grad_top_low, full_down, preferred_element_type=jnp.float32)
    (grad_hidden,) = act_back(grad_act)
    grad_hidden_low = grad_hidden.astype(jnp.bfloat16)
    grad_up = jnp.einsum(
        "td,tf->df", normed_two_low, grad_hidden_low, preferred_element_type=jnp.float32
    )
    grad_normed_two = jnp.einsum(
        "tf,df->td", grad_hidden_low, full_up, preferred_element_type=jnp.float32
    )
    grad_mid_norm, grad_gain_two, grad_bias_two = norm_two_back(grad_normed_two)
    grad_middle = grad_top + grad_mid_norm
    grad_middle_low = grad_middle.astype(jnp.bfloat16)
    grad_out = jnp.einsum(
        "tc,td->cd", attended_low, grad_middle_low, preferred_element_type=jnp.float32
    )
    grad_att = jnp.einsum(
        "td,cd->tc", grad_middle_low, full_out, preferred_element_type=jnp.float32
    )
    grad_att_low = grad_att.astype(jnp.bfloat16)
    grad_att_heads = grad_att_low.reshape(tok_rows, head_count, head_size)
    offsets = jnp.sum(
        (grad_att_low.astype(jnp.float32) * attended).reshape(tok_rows, head_count, head_size),
        axis=2,
    ).T

    def backward_block(operands, source):

        def backward_work(inner):
            grad_query, grad_key, grad_value, key_now, value_now = inner
            key_heads = key_now.reshape(tok_rows, head_count, head_size)
            value_heads = value_now.reshape(tok_rows, head_count, head_size)
            probs = jnp.exp(scores_of(key_now, source) - log_total[:, :, None])
            probs_low = probs.astype(jnp.bfloat16)
            grad_value = grad_value + jnp.einsum(
                "hqk,qhd->khd", probs_low, grad_att_heads, preferred_element_type=jnp.float32
            ).reshape(tok_rows, model_width)
            grad_probs = jnp.einsum(
                "qhd,khd->hqk", grad_att_heads, value_heads, preferred_element_type=jnp.float32
            )
            grad_scores = (probs * (grad_probs - offsets[:, :, None])).astype(jnp.bfloat16)
            grad_query = (
                grad_query
                + jnp.einsum(
                    "hqk,khd->qhd", grad_scores, key_heads, preferred_element_type=jnp.float32
                ).reshape(tok_rows, model_width)
                * scale
            )
            grad_key = (
                grad_key
                + jnp.einsum(
                    "hqk,qhd->khd", grad_scores, query_heads, preferred_element_type=jnp.float32
                ).reshape(tok_rows, model_width)
                * scale
            )
            return (grad_query, grad_key, grad_value, key_now, value_now)

        def backward_keep(inner):
            return inner

        return lax.cond(source <= my_place, backward_work, backward_keep, operands)

    def backward_step(step, carry):
        source = (my_place - step) % blocks_seq
        grad_query, grad_key, grad_value, key_block, value_block = backward_block(carry, source)
        key_block, value_block = passed_along((key_block, value_block), "seq", 1)
        grad_key, grad_value = (
            shifted(grad_key.astype(jnp.bfloat16), "seq", 1).astype(grad_key.dtype),
            shifted(grad_value.astype(jnp.bfloat16), "seq", 1).astype(grad_value.dtype),
        )
        return (grad_query, grad_key, grad_value, key_block, value_block)

    zero_rows = jnp.zeros((tok_rows, model_width), jnp.float32)
    grad_query, grad_key, grad_value, _, _ = lax.fori_loop(
        0, blocks_seq, backward_step, (zero_rows, zero_rows, zero_rows, key_low, value_low)
    )
    grad_proj_low = jnp.concatenate([grad_query, grad_key, grad_value], axis=1).astype(jnp.bfloat16)
    grad_qkv = jnp.einsum(
        "tc,tk->ck", normed_low, grad_proj_low, preferred_element_type=jnp.float32
    )
    grad_normed = jnp.einsum(
        "tk,ck->tc", grad_proj_low, full_qkv, preferred_element_type=jnp.float32
    )
    grad_in_norm, grad_gain_one, grad_bias_one = norm_one_back(grad_normed)
    input_grad = (grad_middle + grad_in_norm)[None]
    part_qkv, part_out, part_up, part_down = (
        lax.psum_scatter(
            grad_qkv.astype(jnp.bfloat16), "seg", scatter_dimension=0, tiled=True
        ).astype(jnp.float32),
        lax.psum_scatter(
            grad_out.astype(jnp.bfloat16), "seg", scatter_dimension=0, tiled=True
        ).astype(jnp.float32),
        lax.psum_scatter(
            grad_up.astype(jnp.bfloat16), "seg", scatter_dimension=0, tiled=True
        ).astype(jnp.float32),
        lax.psum_scatter(
            grad_down.astype(jnp.bfloat16), "seg", scatter_dimension=0, tiled=True
        ).astype(jnp.float32),
    )
    sum_qkv, sum_out, sum_up, sum_down = (
        lax.psum_scatter(
            part_qkv.astype(jnp.bfloat16), "seq", scatter_dimension=1, tiled=True
        ).astype(jnp.float32),
        lax.psum_scatter(
            part_out.astype(jnp.bfloat16), "seq", scatter_dimension=1, tiled=True
        ).astype(jnp.float32),
        lax.psum_scatter(
            part_up.astype(jnp.bfloat16), "seq", scatter_dimension=1, tiled=True
        ).astype(jnp.float32),
        lax.psum_scatter(
            part_down.astype(jnp.bfloat16), "seq", scatter_dimension=1, tiled=True
        ).astype(jnp.float32),
    )
    sum_gain_one, sum_bias_one, sum_gain_two, sum_bias_two = lax.psum(
        (grad_gain_one, grad_bias_one, grad_gain_two, grad_bias_two), ("seq", "seg")
    )
    return (
        result,
        input_grad,
        sum_gain_one,
        sum_bias_one,
        sum_qkv,
        sum_out,
        sum_gain_two,
        sum_bias_two,
        sum_up,
        sum_down,
    )


MESH = pl.DeviceIdType.MESH
BF = jnp.bfloat16
F32 = jnp.float32
def dot_nn(a, b):
    return lax.dot_general(a, b, (((1,), (0,)), ((), ())), preferred_element_type=F32)


def dot_nt(a, b):
    return lax.dot_general(a, b, (((1,), (1,)), ((), ())), preferred_element_type=F32)


def dot_tn(a, b):
    return lax.dot_general(a, b, (((0,), (0,)), ((), ())), preferred_element_type=F32)


def remote(src, dst, send, recv, **place):
    return pltpu.make_async_remote_copy(
        src_ref=src, dst_ref=dst, send_sem=send, recv_sem=recv, device_id=place, device_id_type=MESH
    )


def norm_parts(values):
    center = values - jnp.mean(values, axis=-1, keepdims=True)
    spread = jnp.mean(center * center, axis=-1, keepdims=True)
    inverse = lax.rsqrt(spread + 1e-05)
    return center * inverse, inverse


def greet(q, s, transposed=False):
    y, c = s // 2, s % 2
    barrier = pltpu.get_barrier_semaphore()

    def signal(seq, seg):
        pl.semaphore_signal(barrier, 1, device_id={"seq": seq, "seg": seg}, device_id_type=MESH)

    for d in range(1, 8):
        for core in range(2):
            signal(lax.rem(q + d, 8), 2 * y + core)
    for d in range(1, 4):
        signal(q, lax.rem(s + d, 4))
    if transposed:
        turned = s != q // 2

        @pl.when(turned)
        def _():
            signal(2 * s + q % 2, q // 2)

        return lambda: pl.semaphore_wait(barrier, jnp.where(turned, 18, 17))
    return lambda: pl.semaphore_wait(barrier, 17)


def first_columns(lens, base, rows):
    place = base + lax.broadcasted_iota(jnp.int32, (rows, 1), 0)
    start = jnp.zeros((rows, 1), jnp.int32)
    bound = jnp.zeros((1, 1), jnp.int32)
    for i in range(lens.shape[0]):
        bound = bound + lens[i : i + 1, 0:1]
        start = jnp.where(place >= bound, bound, start)
    return start


def seen_mask(start, base_q, base_k, rows, columns):
    place = base_q + lax.broadcasted_iota(jnp.int32, (rows, columns), 0)
    key = base_k + lax.broadcasted_iota(jnp.int32, (rows, columns), 1)
    return (key <= place) & (key >= start)


def rows(k, n):
    return pl.ds(k * n if isinstance(k, int) else pl.multiple_of(k * n, n), n)


def lanes(k, n=128):
    return pl.ds(pl.multiple_of(k * n, n), n)


T = 256
HALF = 128


def places(z, x):
    zn, zc = z + 1 - 2 * (z % 2), (z + 2) % 4
    znc = (zn + 2) % 4
    here, near_z, near_x, cross = 2 * z + x, 2 * zn + x, 2 * z + 1 - x, 2 * zc + x
    blocks = (here, near_x, near_z, cross, 2 * znc + x, 2 * zc + 1 - x, 2 * zn + 1 - x, 2 * znc + 1 - x)
    return here, near_z, near_x, cross, blocks


def nth(values, k):
    out = values[0]
    for i, value in enumerate(values[1:], 1):
        out = jnp.where(k == i, value, out)
    return out


VM = pl.BlockSpec(memory_space=pltpu.VMEM)
HB = pl.BlockSpec(memory_space=pl.ANY)
S = jax.ShapeDtypeStruct
SM = pl.BlockSpec(memory_space=pltpu.SMEM)


def gelu_parts(u):
    root = math.sqrt(2.0 / math.pi)
    square = u * u
    t = jnp.tanh(root * (u + 0.044715 * (square * u)))
    value = 0.5 * u * (1.0 + t)
    slope = 0.5 * (1.0 + t) + 0.5 * u * (1.0 - t * t) * (root * (1.0 + 0.134145 * square))
    return value, slope


def norm_back(grad, gain, unit, inverse):
    through = grad * gain
    a = jnp.mean(through, axis=-1, keepdims=True)
    b = jnp.mean(through * unit, axis=-1, keepdims=True)
    return inverse * (through - a - unit * b)


def layer_kernel(
    x_ref, lens_ref, g_ref, wo_ref, gain_ref, bias_ref, gain2_ref, bias2_ref, wq_hbm, wu_hbm, wd_hbm,
    result_out, dx_v, fin_r, gq_r, gout_out, up_r, gdown_out, sums_out, xs_hbm, h1_hbm,
    g_v, wu_v, wd_v, wo_v, o_v, qkv_v, of_v, lse_v, wh_v, load_sem,
    keep_sem, ob, wq_s, lens_s, lens_r, qs, qr, ws, wr, xs_send, xs_recv, xu_recv, os_send, os_recv,
    middle, h2, big, mine, near_s, near_r, twin_s, twin_r, far_keep, far_s, far_r, do_v,
    hs, hr, ns, nr, ts, tr, fs, fr,
    pack, x_r, z_r, up_s, gxs, gxr, gzs, gzr, ups, upr,
    oc_r, oy_r, ox_r, oz_r, oo_r, cs, cr,
    doh, dq, dk, dv, dos, dor,
    fin_s, dcs, dcr, sts, str_, fns, fnr,
    gq, gq_b, gq_y, gqs, gqr,
    vec, vec_r, vs, vr,
):
    q, s = lax.axis_index("seq"), lax.axis_index("seg")
    z, x = q // 2, q % 2
    y, c = s // 2, s % 2
    sib = s + 1 - 2 * c
    across = (1 - y) * 2 + c
    corner = (1 - y) * 2 + 1 - c
    group = z // 2
    head = 4 * (z % 2) + 2 * x + c
    other_head = head + 1 - 2 * c
    home = c == group
    away = jnp.logical_not(home)
    column = 2 * y + group
    here, near_z, near_x, cross, blocks = places(z, x)
    scale = 1.0 / math.sqrt(HEAD_DIM)

    met = greet(q, s, True)

    picks = tuple(
        pltpu.make_async_copy(
            wq_hbm.at[:, lanes(8 * j + of_head)], wq_s.at[k, :, j * 128 : (j + 1) * 128], load_sem.at[10 + 3 * k + j]
        )
        for k, of_head in enumerate((head, other_head))
        for j in range(3)
    )
    loads = tuple(
        pltpu.make_async_copy(src, dst, load_sem.at[k])
        for k, (src, dst) in enumerate(((wd_hbm, wd_v), (wu_hbm.at[:, lanes(s, 1024)], wu_v.at[rows(s, T)])))
    )
    for copy in picks + loads:
        copy.start()
    for k in range(lens_ref.shape[1]):
        lens_s[k : k + 1] = jnp.full((1, 128), lens_ref[0, k], jnp.int32)

    @pl.when(home)
    def _():
        big[rows(q, T)] = x_ref[...]

    for copy in picks:
        copy.wait()
    wh_v[rows(s, T)] = wq_s[0]
    met()

    def half_rows(b, part):
        return big.at[pl.ds(pl.multiple_of(b * T + part * HALF, HALF), HALF)]

    def over_copy(part):
        src = x_ref.at[part * HALF : (part + 1) * HALF]
        return remote(src, half_rows(q, part), xs_send.at[24 + part], xs_recv.at[q], seq=cross, seg=2 * y + part)

    def twin_copy(part, recv, k):
        return remote(half_rows(q, part), half_rows(q, part), xs_send.at[24 + k], recv.at[q], seg=sib)

    twin_track, twin_rest = twin_copy(1 - c, xs_recv, 0), twin_copy(c, xu_recv, 1)

    @pl.when(home)
    def _():
        twin_track.start()
        twin_rest.start()

    @pl.when(jnp.logical_not(home))
    def _():
        over_copy(0).start()
        over_copy(1).start()

    mine_wh = wh_v.at[rows(s, T)]
    q_across = remote(wq_s.at[0], mine_wh, qs.at[0], qr.at[0], seg=across)
    q_sib = remote(wq_s.at[1], mine_wh, qs.at[1], qr.at[1], seg=sib)
    q_corner = remote(wq_s.at[1], mine_wh, qs.at[2], qr.at[2], seg=corner)
    l_sib = remote(lens_s, lens_r, qs.at[3], qr.at[3], seg=sib)
    first = (q_across, q_corner, q_sib, l_sib)
    for copy in first:
        copy.start()

    def x_copy(b, k, recv, **to):
        src = half_rows(b, c)
        return remote(src, src, xs_send.at[k], recv.at[b], **to)

    own_z, own_x = x_copy(q, 0, xs_recv, seq=near_z), x_copy(q, 8, xs_recv, seq=near_x)

    @pl.when(jnp.logical_not(home))
    def _():
        x_copy(q, 0, xs_recv, seq=q).wait_recv()

    own_z.start()
    own_x.start()

    def u_part(seg, part):
        return wu_v.at[pl.ds(pl.multiple_of(seg * T + part * HALF, HALF), HALF)]

    def o_part(seg, part):
        return wo_v.at[pl.ds(pl.multiple_of(seg * T + part * HALF, HALF), HALF)]

    u_far = tuple(
        remote(
            wu_hbm.at[pl.ds(pl.multiple_of(x * HALF, HALF), HALF), lanes(to, 1024)], u_part(s, x), ws.at[k], wr.at[k],
            seg=to,
        )
        for k, to in ((0, across), (1, corner))
    )
    u_over = tuple(
        remote(u_part(of_seg, x), u_part(of_seg, x), ws.at[11 + k], wr.at[11 + k], seq=near_x)
        for k, of_seg in ((0, across), (1, corner))
    )
    u_sib = remote(wu_hbm.at[:, lanes(sib, 1024)], wu_v.at[rows(s, T)], ws.at[2], wr.at[2], seg=sib)
    o_far = remote(
        wo_ref.at[pl.ds(pl.multiple_of(x * HALF, HALF), HALF)], o_part(s, x), ws.at[3], wr.at[3], seg=across
    )
    o_over = remote(o_part(across, x), o_part(across, x), ws.at[13], wr.at[13], seq=near_x)
    o_sib = remote(wo_ref, wo_v.at[rows(s, T)], ws.at[4], wr.at[4], seg=sib)
    o_pass = tuple(
        remote(o_part(across, part), o_part(across, part), ws.at[k], wr.at[k], seg=sib)
        for k, part in ((5, x), (14, 1 - x))
    )
    g_rows = lambda k, part: g_v.at[pl.ds(2 * T + part * T + k * HALF, HALF)]
    g_across = tuple(
        remote(g_ref.at[k * HALF : (k + 1) * HALF], g_rows(0, k), ws.at[6 + k], wr.at[6 + k], seg=across)
        for k in range(2)
    )
    g_sib = remote(g_ref, g_v.at[T : 2 * T], ws.at[8], wr.at[8], seg=sib)
    g_pass = tuple(remote(g_rows(0, k), g_rows(1, k), ws.at[9 + k], wr.at[9 + k], seg=sib) for k in range(2))
    wo_v[rows(s, T)] = wo_ref[...]
    g_v[0:T] = g_ref[...]
    for copy in u_far + (o_far,) + g_across:
        copy.start()
    for copy in first:
        copy.wait_recv()
    lens = jnp.where(home, lens_s[...], lens_r[...])

    gain, bias = gain_ref[...], bias_ref[...]

    def keep(b):
        at = rows(b, T)
        return (
            pltpu.make_async_copy(big.at[at], xs_hbm.at[at], keep_sem.at[b]),
            pltpu.make_async_copy(pack.at[b], h1_hbm.at[at], keep_sem.at[8 + b]),
        )

    def project(b):
        unit, _ = norm_parts(big[rows(b, T)].astype(F32))
        low = (unit * gain + bias).astype(BF)
        pack[b] = low
        qkv_v[rows(b, T)] = dot_nn(low, wh_v[...]).astype(BF)
        for copy in keep(b):
            copy.start()

    def track_step(k, _):
        b = nth(blocks, k)

        @pl.when(k < 8)
        def _():
            x_copy(b, 0, xs_recv, seq=q).wait_recv()

        @pl.when((k == 1) | (k == 3))
        def _():
            x_copy(b, k, xs_recv, seq=near_z).start()

        @pl.when((k == 3) | (k == 4))
        def _():
            x_copy(b, 8 + k, xs_recv, seq=near_x).start()

        @pl.when(k < 8)
        def _():
            x_copy(b, 16 + k, xu_recv, seg=sib).start()

        last = nth(blocks, k - 1)

        @pl.when((k > 1) | jnp.logical_not(home))
        def _():
            x_copy(last, 0, xu_recv, seg=sib).wait_recv()

        project(last)

        return 0

    lax.fori_loop(1, 6, track_step, 0)
    for arrived, copy in zip(u_far, u_over):
        arrived.wait_recv()
        copy.start()
    lax.fori_loop(6, 9, track_step, 0)
    o_far.wait_recv()
    o_over.start()
    o_pass[0].start()
    for copy in (u_sib, o_sib, g_sib):
        copy.start()

    def o_copy(i, sender):
        return remote(
            ob.at[i // 4, (i // 2) % 2, i % 2], o_v.at[:, lanes(sender)], os_send.at[i], os_recv.at[sender], seq=i, seg=column
        )

    o_mine = pltpu.make_async_copy(ob.at[group, z % 2, x], o_v.at[:, lanes(head)], os_recv.at[head])
    for i in (4, 5, 6, 7, 0, 1, 2, 3):
        n = (i + 1) * T
        start = first_columns(lens, i * T, T)
        scores = dot_nt(qkv_v[i * T : n, :128], qkv_v[:n, 128:256]) * scale
        scores = jnp.where(seen_mask(start, i * T, 0, T, n), scores, -1e30)
        top = jnp.max(scores, axis=1, keepdims=True)
        weights = jnp.exp(scores - top)
        total = jnp.sum(weights, axis=1, keepdims=True)
        mixed = dot_nn(weights.astype(BF), qkv_v[:n, 256:384]) / total
        of_v[i * T : n] = mixed
        lse_v[:, i : i + 1] = top + jnp.log(total)
        ob[i // 4, (i // 2) % 2, i % 2] = mixed.astype(BF)
        here = (q == i) & home

        @pl.when(jnp.logical_not(here))
        def _():
            o_copy(i, head).start()

        @pl.when(here)
        def _():
            o_mine.start()

    o_over.wait_recv()
    o_pass[1].start()
    for arrived, copy in zip(g_across, g_pass):
        arrived.wait_recv()
        copy.start()

    for i in range(8):
        o_copy(i, i).wait_recv()
    for copy in o_pass + (o_sib,):
        copy.wait_recv()

    value = x_ref[...].astype(F32) + dot_nn(o_v[...], wo_v[...])
    middle[...] = value
    unit, _ = norm_parts(value)
    h2[0:T] = (unit * gain2_ref[...] + bias2_ref[...]).astype(BF)

    def far_rows(ref, part, k):
        return ref.at[pl.ds(2 * T + k * T + part * HALF, HALF)]

    h_far = tuple(
        remote(h2.at[k * HALF : (k + 1) * HALF], far_rows(h2, 0, k), hs.at[k], hr.at[k], seg=across)
        for k in range(2)
    )
    h_pass = tuple(
        remote(far_rows(h2, 0, k), far_rows(h2, 1, k), hs.at[2 + k], hr.at[2 + k], seg=sib) for k in range(2)
    )
    h_sib = remote(h2.at[0:T], h2.at[T : 2 * T], hs.at[4], hr.at[4], seg=sib)
    for copy in h_far + (h_sib,):
        copy.start()
    for copy in loads:
        copy.wait()
    for copy in u_over + g_pass + (u_sib, g_sib):
        copy.wait_recv()
    for b in range(8):
        for copy in keep(b):
            copy.wait()
    for k in range(1, 8):
        if k in (1, 3):
            x_copy(blocks[k], k, xs_recv, seq=near_z).wait_send()
        if k in (3, 4):
            x_copy(blocks[k], 8 + k, xs_recv, seq=near_x).wait_send()
        x_copy(blocks[k], 16 + k, xu_recv, seg=sib).wait_send()

    @pl.when(home)
    def _():
        twin_track.wait_send()
        twin_rest.wait_send()

    @pl.when(jnp.logical_not(home))
    def _():
        over_copy(0).wait_send()
        over_copy(1).wait_send()

    for i in range(8):
        @pl.when(jnp.logical_not((q == i) & home))
        def _():
            o_copy(i, head).wait_send()

    for copy in first + u_far + u_over + o_pass + g_across + g_pass + (u_sib, o_far, o_over, o_sib, g_sib, own_z, own_x):
        copy.wait_send()

    def work(part):
        at = slice(part * T, (part + 1) * T)
        value, slope = gelu_parts(dot_nn(h2[at], wu_v[...]))
        low = value.astype(BF)
        big[at] = low
        du = (slope * dot_nt(g_v[at], wd_v[...])).astype(BF)
        big[4 * T + part * T : 4 * T + (part + 1) * T] = du
        return dot_nt(du, wu_v[...]), dot_nn(low, wd_v[...])

    near = tuple(remote(near_s.at[k], near_r.at[k], ns.at[k], nr.at[k], seg=sib) for k in range(2))
    twin = tuple(
        tuple(remote(twin_s.at[k, n], twin_r.at[k, n], ts.at[2 * k + n], tr.at[2 * k + n], seg=sib) for n in range(2))
        for k in range(2)
    )
    far = tuple(
        tuple(remote(far_s.at[k, n], far_r.at[k, n], fs.at[2 * k + n], fr.at[2 * k + n], seg=across) for n in range(2))
        for k in range(2)
    )

    def send_twin(n, parts):
        for k in range(2):
            far_keep[k] = parts[k][:HALF]
            twin_s[k, n] = parts[k][HALF:].astype(BF)
            twin[k][n].start()

    def send_far(n):
        for k in range(2):
            twin[k][n].wait_recv()
            far_s[k, n] = (far_keep[k] + twin_r[k, n].astype(F32)).astype(BF)
            if k == 0:
                far[k][n].start()

    parts = work(0)
    for k in range(2):
        mine[k] = parts[k]
    h_sib.wait_recv()
    parts = work(1)
    for k in range(2):
        near_s[k] = parts[k].astype(BF)
        near[k].start()
    h_far[0].wait_recv()
    h_pass[0].start()
    h_pass[0].wait_recv()
    send_twin(0, work(2))
    h_far[1].wait_recv()
    h_pass[1].start()
    send_far(0)
    h_pass[1].wait_recv()
    send_twin(1, work(3))
    send_far(1)

    def gx_copy(d):
        return remote(pack.at[2 * d + 1 - x], x_r.at[d], gxs.at[d], gxr.at[d], seq=near_x)

    zn, zc = z + 1 - 2 * (z % 2), (z + 2) % 4
    znc = (zn + 2) % 4

    def pack_rows(k, _):
        d = nth((znc, zc, zn, z), k)
        up = dot_tn(h2[:, lanes(d, T)], big[4 * T :]).astype(BF)
        down = dot_tn(big[: 4 * T], g_v[:, lanes(d, T)]).astype(BF)
        for e in range(2):
            pack[2 * d + e, :, :512] = up[:, e * 512 : (e + 1) * 512]
            for j in range(4):
                pack[2 * d + e, :, 512 + j * 128 : 640 + j * 128] = down[
                    j * T : (j + 1) * T, e * 128 : (e + 1) * 128
                ]

        @pl.when(k < 1)
        def _():
            gx_copy(d).start()

        return 0

    lax.fori_loop(0, 4, pack_rows, 0)

    near[0].wait_recv()
    far[0][0].wait_recv()
    far[0][1].wait_recv()
    grad = mine[0] + near_r[0].astype(F32) + jnp.concatenate([far_r[0, 0], far_r[0, 1]], axis=0).astype(F32)
    unit, inverse = norm_parts(middle[...])
    vec[...] = jnp.zeros_like(vec)
    vec[2:3] = jnp.sum(grad * unit, axis=0, keepdims=True)
    vec[3:4] = jnp.sum(grad, axis=0, keepdims=True)
    dx = g_v[0:T].astype(F32) + norm_back(grad, gain2_ref[...], unit, inverse)
    dx_v[...] = dx
    dy = dx.astype(BF)
    do_v[...] = dot_nt(dy, wo_v[...]).astype(BF)

    def do_copy(h, block):
        return remote(
            do_v.at[:, h * 128 : (h + 1) * 128], doh.at[rows(block, T)], dos.at[h], dor.at[block],
            seq=2 * (2 * c + h // 4) + (h // 2) % 2, seg=2 * y + h % 2,
        )

    do_mine = pltpu.make_async_copy(do_v.at[:, lanes(head)], doh.at[rows(q, T)], dor.at[q])
    for h in range(8):
        self_too = (head == h) & home

        @pl.when(jnp.logical_not(self_too))
        def _():
            do_copy(h, q).start()

        @pl.when(self_too)
        def _():
            do_mine.start()

    for copy in h_far + h_pass + (h_sib,):
        copy.wait_send()
    h2[...] = dot_tn(o_v[...], dy).astype(BF)

    def out_rows(part, core):
        return h2.at[rows(2 * part + core, T)]

    out_core = tuple(remote(out_rows(k, 1 - c), oc_r.at[k], cs.at[5 + k], cr.at[5 + k], seg=sib) for k in range(2))
    for copy in out_core:
        copy.start()
    for part in range(2):
        out_core[part].wait_recv()
        oc_r[part] = (oc_r[part].astype(F32) + out_rows(part, c)[...].astype(F32)).astype(BF)
    out_y = remote(oc_r.at[1 - y], oy_r, cs.at[1], cr.at[1], seg=across)
    out_y.start()
    far[1][0].start()
    far[1][1].start()

    def come(into, recv, slot):
        return remote(into.at[slot], into.at[slot], recv.at[slot], recv.at[slot], seq=near_x)

    def gz_copy(k, d, to):
        return remote(x_r.at[d], z_r.at[k], gzs.at[k], gzr.at[k], seq=to)

    gz = (gz_copy(0, znc, near_z), gz_copy(1, zn, near_z), gz_copy(2, zc, cross))

    def pack_sum(d):
        gx_copy(d).wait_recv()
        return pack[2 * d + x].astype(F32) + x_r[d].astype(F32)

    x_r[znc] = pack_sum(znc).astype(BF)
    gz[0].start()
    gx_copy(zc).start()

    dk[...] = jnp.zeros_like(dk)
    dv[...] = jnp.zeros_like(dv)
    for i in range(8):
        do_copy(0, i).wait_recv()
        top = i * T
        start = first_columns(lens, top, T)
        query = qkv_v[top : top + T, :128]
        grad = doh[top : top + T]
        delta = jnp.sum(grad.astype(F32) * of_v[top : top + T], axis=1, keepdims=True)
        log_total = lse_v[:, i : i + 1]
        total = jnp.zeros((T, 128), F32)
        for base in range(0, top + T, 1024):
            n = min(1024, top + T - base)
            keys = qkv_v[base : base + n, 128:256]
            probs = jnp.exp(dot_nt(query, keys) * scale - log_total)
            probs = jnp.where(seen_mask(start, top, base, T, n), probs, 0.0)
            dp = dot_nt(grad, qkv_v[base : base + n, 256:384])
            ds = (probs * (dp - delta)).astype(BF)
            dv[base : base + n] += dot_tn(probs.astype(BF), grad)
            dk[base : base + n] += dot_tn(ds, query)
            total += dot_nn(ds, keys)
        dq[top : top + T] = total

    gz[0].wait_recv()
    x_r[zc] = (pack_sum(zc) + z_r[0].astype(F32)).astype(BF)
    gz[2].start()

    gq[...] = jnp.zeros_like(gq)
    own_a, other_xa, other_za, own_b, other_zb, other_xb, diag_a, diag_b = blocks
    order = (diag_a, diag_b, other_za, other_xb, other_xa, other_zb, own_a, own_b)

    def x_load(i):
        return pltpu.make_async_copy(xs_hbm.at[rows(nth(order, i), T)], wu_v.at[rows(i % 2, T)], load_sem.at[2 + i % 2])

    def h_load(i):
        return pltpu.make_async_copy(h1_hbm.at[rows(nth(order, i), T)], wu_v.at[rows(2 + i % 2, T)], load_sem.at[4 + i % 2])

    def dhc_copy(b):
        return remote(
            big.at[pl.ds(pl.multiple_of(b * T + (1 - c) * HALF, HALF), HALF)], wo_v.at[rows(b, HALF)], dcs.at[b], dcr.at[b], seg=sib
        )

    def half(b):
        return big.at[pl.ds(pl.multiple_of(b * T + c * HALF, HALF), HALF)]

    def step_copy(k, b, to):
        return remote(wo_v.at[rows(b, HALF)], wd_v.at[rows(k, HALF)], sts.at[k], str_.at[k], seq=to)

    steps = (
        step_copy(0, diag_a, near_z), step_copy(1, diag_b, near_x), step_copy(2, other_za, near_z),
        step_copy(3, other_xb, near_x), step_copy(4, other_xa, near_x), step_copy(5, other_zb, near_z),
    )
    x_load(0).start()
    h_load(0).start()

    def grads_at(at):
        return jnp.concatenate([dq[at] * scale, dk[at] * scale, dv[at]], axis=1).astype(BF)

    def block_step(i, _):
        @pl.when(i < 8)
        def _():
            b = nth(order, i)

            at = rows(b, T)
            big[at] = dot_nt(grads_at(at), wh_v[...]).astype(BF)
            dhc_copy(b).start()

        @pl.when(i > 0)
        def _():
            b = nth(order, i - 1)
            dhc_copy(b).wait_recv()
            wo_v[rows(b, HALF)] = (half(b)[...].astype(F32) + wo_v[rows(b, HALF)].astype(F32)).astype(BF)
            for k in range(4):
                @pl.when(i == k + 1)
                def _():
                    steps[k].start()

        return 0

    lax.fori_loop(0, 9, block_step, 0)
    gx_copy(zn).start()

    def sum_step(i, _):
        @pl.when(i < 7)
        def _():
            x_load(i + 1).start()
            h_load(i + 1).start()

        at = rows(nth(order, i), T)
        dh = big[at].astype(F32)
        x_load(i).wait()
        h_load(i).wait()
        gq[...] += dot_tn(wu_v[rows(2 + i % 2, T)], grads_at(at))
        unit, _ = norm_parts(wu_v[rows(i % 2, T)].astype(F32))
        vec[0:1] += jnp.sum(dh * unit, axis=0, keepdims=True)
        vec[1:2] += jnp.sum(dh, axis=0, keepdims=True)
        return 0

    lax.fori_loop(0, 8, sum_step, 0)
    for k, b in ((5, other_zb), (4, other_xa)):
        steps[k - 4].wait_recv()
        wo_v[rows(b, HALF)] = (wo_v[rows(b, HALF)].astype(F32) + wd_v[(k - 4) * HALF : (k - 3) * HALF].astype(F32)).astype(BF)
        steps[k].start()

    x_r[zn] = pack_sum(zn).astype(BF)
    gz[1].start()

    out_y.wait_recv()
    out = (oc_r[y].astype(F32) + oy_r[...].astype(F32)).astype(BF)
    for k in range(8):
        ob[k // 4, (k // 2) % 2, k % 2] = out[:, k * 128 : (k + 1) * 128]
    out_x = remote(ob.at[:, :, 1 - x], ox_r, cs.at[2], cr.at[2], seq=near_x)
    out_x.start()
    gx_copy(z).start()

    gq_b[...] = gq[...].astype(BF).reshape(2, 2, T, 384)
    q_y = remote(gq_b.at[1 - y], gq_y, gqs.at[0], gqr.at[0], seg=across)
    q_y.start()
    v_core = remote(vec, vec_r.at[0], vs.at[8], vr.at[8], seg=sib)
    v_core.start()
    v_core.wait()
    vec[...] += vec_r[0]
    v_y = remote(vec, vec_r.at[1], vs.at[9], vr.at[9], seg=across)
    v_y.start()
    def fin_sum(k, b, pair):
        for n in pair:
            steps[n].wait_recv()
        fin_s[k] = (
            wo_v[rows(b, HALF)].astype(F32) + wd_v[rows(pair[0], HALF)].astype(F32)
            + wd_v[rows(pair[1], HALF)].astype(F32)
        ).astype(BF)

    fin_over = remote(fin_s.at[1], fin_r.at[c], fns.at[0], fnr.at[c], seq=cross, seg=column)
    fin_twin = remote(fin_s.at[0], fin_r.at[c], fns.at[1], fnr.at[c], seg=sib)
    fin_own = pltpu.make_async_copy(fin_s.at[0], fin_r.at[c], fnr.at[c])
    fin_sum(1, own_b, (3, 5))
    fin_over.start()
    fin_sum(0, own_a, (2, 4))

    @pl.when(away)
    def _():
        fin_twin.start()

    @pl.when(home)
    def _():
        fin_own.start()

    v_y.wait()
    vec[...] += vec_r[1]

    def v_copy(b, sender):
        return remote(vec, vec_r.at[2 + sender], vs.at[b], vr.at[sender], seq=b)

    for b in range(8):
        @pl.when(q != b)
        def _():
            v_copy(b, q).start()

    q_y.wait_recv()
    gq_y[...] = (gq_y[...].astype(F32) + gq_b[y].astype(F32)).astype(BF)

    def column_copy(part, j):
        place = 8 * j + head
        owner, slot = place // 3, place % 3
        src = gq_y.at[part, :, j * 128 : (j + 1) * 128]
        copy = remote(
            src, gq_r.at[slot, group], gqs.at[1 + 3 * part + j], gqr.at[1 + 2 * slot + group],
            seq=owner, seg=2 * y + part,
        )
        local = pltpu.make_async_copy(src, gq_r.at[slot, group], gqr.at[1 + 2 * slot + group])
        return (owner == q) & (c == part), copy, local

    columns = tuple(column_copy(part, j) for part in range(2) for j in range(3))
    out_x.wait_recv()
    ox_r[...] = (ox_r[...].astype(F32) + ob[:, :, x].astype(F32)).astype(BF)
    out_z = remote(ox_r.at[:, 1 - z % 2], oz_r, cs.at[3], cr.at[3], seq=near_z)
    out_z.start()
    for self_too, copy, local in columns:
        @pl.when(jnp.logical_not(self_too))
        def _():
            copy.start()

        @pl.when(self_too)
        def _():
            local.start()

    out_z.wait_recv()
    oz_r[...] = (oz_r[...].astype(F32) + ox_r[:, z % 2].astype(F32)).astype(BF)
    out_o = remote(oz_r.at[1 - group], oo_r, cs.at[4], cr.at[4], seq=cross)
    out_o.start()

    total = pack_sum(z)
    for k in (1, 2):
        gz[k].wait_recv()
        total = total + z_r[k].astype(F32)
    up_s[...] = total[:, :512].astype(BF)
    turned = s != z
    up_turn = remote(up_s, up_r, ups, upr, seq=2 * s + x, seg=z)
    up_own = pltpu.make_async_copy(up_s, up_r, upr)

    @pl.when(turned)
    def _():
        up_turn.start()

    @pl.when(jnp.logical_not(turned))
    def _():
        up_own.start()

    for j in range(4):
        gdown_out[j * T : (j + 1) * T] = total[:, 512 + j * 128 : 640 + j * 128]
    vec_r[2 + q] = vec[...]
    for b in range(8):
        @pl.when(q != b)
        def _():
            v_copy(b, b).wait_recv()

    vec_sum = vec_r[2]
    for b in range(1, 8):
        vec_sum = vec_sum + vec_r[2 + b]
    out_o.wait_recv()
    gout_out[...] = oz_r[group].astype(F32) + oo_r[...].astype(F32)
    sums_out[...] = vec_sum
    for slot in range(3):
        for part in range(2):
            pltpu.make_async_copy(gq_r.at[slot, part], gq_r.at[slot, part], gqr.at[1 + 2 * slot + part]).wait()
    near[1].wait_recv()
    far[1][0].wait_recv()
    far[1][1].wait_recv()
    result_out[...] = (
        middle[...] + mine[1] + near_r[1].astype(F32)
        + jnp.concatenate([far_r[1, 0], far_r[1, 1]], axis=0).astype(F32)
    ).astype(BF)
    for k in range(2):
        come(fin_r, fnr, k).wait_recv()
    up_own.wait()

    for h in range(8):
        @pl.when(jnp.logical_not((head == h) & home))
        def _():
            do_copy(h, q).wait_send()

    for b in range(8):
        dhc_copy(b).wait_send()

        @pl.when(q != b)
        def _():
            v_copy(b, q).wait_send()

    for d in range(4):
        gx_copy(d).wait_send()
    for copy in out_core + (out_y, out_x, out_z, out_o, q_y, fin_over) + near + steps + gz:
        copy.wait_send()
    for k in range(2):
        for n in range(2):
            twin[k][n].wait_send()
            far[k][n].wait_send()

    @pl.when(away)
    def _():
        fin_twin.wait_send()

    @pl.when(turned)
    def _():
        up_turn.wait_send()

    for self_too, copy, _ in columns:
        @pl.when(jnp.logical_not(self_too))
        def _():
            copy.wait_send()


def layer(x, lens, g, wo, gain, bias, gain2, bias2, wq, wu, wd):
    dma = pltpu.SemaphoreType.DMA
    low = lambda *shape: pltpu.VMEM(shape, BF)
    wide = lambda *shape: pltpu.VMEM(shape, F32)
    return pl.pallas_call(
        layer_kernel,
        out_shape=(
            S((256, 1024), BF), S((256, 1024), F32), S((2, 128, 1024), BF), S((3, 2, 256, 128), BF),
            S((256, 128), F32), S((256, 512), BF), S((1024, 128), F32), S((8, 1024), F32),
            S((2048, 1024), BF), S((2048, 1024), BF),
        ),
        in_specs=[VM, SM] + [VM] * 6 + [HB] * 3,
        out_specs=(VM,) * 8 + (HB,) * 2,
        scratch_shapes=[
            low(1024, 1024), low(1024, 1024), low(1024, 1024), low(1024, 1024), low(256, 1024), low(2048, 384),
            wide(2048, 128), wide(256, 8), low(1024, 384), dma((16,)),
            dma((16,)), low(2, 2, 2, 256, 128), low(2, 256, 384), pltpu.VMEM((8, 128), jnp.int32),
            pltpu.VMEM((8, 128), jnp.int32), dma((4,)), dma((4,)), dma((15,)), dma((15,)),
            dma((26,)), dma((8,)), dma((8,)), dma((8,)), dma((8,)),
            wide(256, 1024), low(1024, 1024), low(2048, 1024), wide(2, 256, 1024),
            low(2, 256, 1024), low(2, 256, 1024), low(2, 2, 128, 1024), low(2, 2, 128, 1024), wide(2, 128, 1024),
            low(2, 2, 128, 1024), low(2, 2, 128, 1024), low(256, 1024),
            dma((5,)), dma((5,)), dma((2,)), dma((2,)), dma((4,)), dma((4,)), dma((4,)), dma((4,)),
            low(8, 256, 1024), low(4, 256, 1024), low(3, 256, 1024), low(256, 512),
            dma((4,)), dma((4,)), dma((3,)), dma((3,)), dma, dma,
            low(2, 256, 1024), low(256, 1024), low(2, 2, 256, 128),
            low(2, 256, 128), low(256, 128), dma((7,)), dma((7,)),
            low(2048, 128), wide(2048, 128), wide(2048, 128), wide(2048, 128), dma((8,)), dma((8,)),
            low(2, 128, 1024),
            dma((8,)), dma((8,)), dma((6,)), dma((6,)), dma((2,)), dma((2,)),
            wide(1024, 384), low(2, 2, 256, 384), low(2, 256, 384),
            dma((7,)), dma((7,)),
            wide(8, 1024), wide(10, 8, 1024), dma((10,)), dma((10,)),
        ],
        compiler_params=pltpu.CompilerParams(
            collective_id=1, has_side_effects=True, vmem_limit_bytes=63 * 2**20
        ),
        cost_estimate=pl.CostEstimate(flops=2 * 10**10, bytes_accessed=40 * 2**20, transcendentals=2 * 2**20),
        name="layer",
    )(x, lens, g, wo, gain, bias, gain2, bias2, wq, wu, wd)


def finish_kernel(
    x_ref, gain_ref, result_ref, dx_ref, fin_ref, gq_ref, out_ref, up_ref, down_ref, sums_ref,
    result, dx, gain_one, bias_one, gqkv, gout, gain_two, bias_two, gup, gdown,
):
    result[...] = result_ref[...]
    unit, inverse = norm_parts(x_ref[...].astype(F32))
    dx[...] = dx_ref[...] + norm_back(fin_ref[0].astype(F32), gain_ref[...], unit, inverse)
    for slot in range(3):
        gqkv[:, slot * 128 : (slot + 1) * 128] = gq_ref[slot, 0].astype(F32) + gq_ref[slot, 1].astype(F32)
    gout[...] = out_ref[...]
    gup[...] = up_ref[...].astype(F32)
    gdown[...] = down_ref[...]
    for k, ref in enumerate((gain_one, bias_one, gain_two, bias_two)):
        ref[...] = sums_ref[k]


def finish(x, gain, *parts):
    line = S((1024,), F32)
    part = lambda r, n: pl.BlockSpec((r // 2, n), lambda i: (i, 0))
    whole = lambda r, n: pl.BlockSpec((r, n), lambda i: (0, 0))
    row = pl.BlockSpec((1024,), lambda i: (0,))
    return pl.pallas_call(
        finish_kernel,
        grid=(2,),
        out_shape=(
            S((256, 1024), BF), S((256, 1024), F32), line, line, S((256, 384), F32), S((256, 128), F32), line, line,
            S((256, 512), F32), S((1024, 128), F32),
        ),
        in_specs=[
            part(256, 1024), whole(1, 1024), part(256, 1024), part(256, 1024),
            pl.BlockSpec((1, 128, 1024), lambda i: (i, 0, 0)),
            pl.BlockSpec((3, 2, 128, 128), lambda i: (0, 0, i, 0)), part(256, 128), part(256, 512), part(1024, 128),
            whole(8, 1024),
        ],
        out_specs=(
            part(256, 1024), part(256, 1024), row, row, part(256, 384), part(256, 128), row, row, part(256, 512),
            part(1024, 128),
        ),
        compiler_params=pltpu.CompilerParams(vmem_limit_bytes=60 * 2**20),
        name="finish",
    )(x, gain, *parts)


def per_device_fast(
    tokens, article_lengths, gain_one, bias_one, w_qkv, w_out, gain_two, bias_two, w_up, w_down, cotangent
):
    x = tokens[0]
    *parts, _, _ = layer(
        x, article_lengths, cotangent[0], w_out, gain_one[None], bias_one[None], gain_two[None], bias_two[None],
        w_qkv, w_up, w_down,
    )
    result, dx, *rest = finish(x, gain_one[None], *parts)
    return (result[None], dx[None], *rest)


def solution(mesh):
    one_pair = mesh.shape["seq"] == HEADS and mesh.shape["seg"] == 4
    return jax.shard_map(
        per_device_fast if one_pair else per_device,
        mesh=mesh,
        in_specs=(
            P("seg", "seq", None),
            P("seg", None),
            P(),
            P(),
            P("seg", None),
            P("seg", None),
            P(),
            P(),
            P("seg", None),
            P("seg", None),
            P("seg", "seq", None),
        ),
        out_specs=(
            P("seg", "seq", None),
            P("seg", "seq", None),
            P(),
            P(),
            P("seg", "seq"),
            P("seg", "seq"),
            P(),
            P(),
            P("seg", "seq"),
            P("seg", "seq"),
        ),
        check_vma=False,
    )
```

profile of v0, /device:TPU:4, one launch (start us, length us, event | category | flops | bytes accessed | tf_op | source)
XLA Modules:
  0.0 197.5 jit_solution(485542882794523870)
XLA Ops:
  0.6 193.1 %layer.1 = (bf16[256,1024]{1,0:T(8,128)(2,1)}, f32[256,1024]{1,0:T(8,128)}, bf16[2,128,1024]{2,1,0:T(8,128)(2,1)}, bf16[3,2,256,128]{3,2,1,0:T(8,128)(2,1)}, f32...) custom-call(bf16[256,1024]{1,0:T(8,128)(2,1)} %bitcast.8, ...), custom_call_target="tpu_custom_call" | custom-call | flops 20000000000 | bytes 41943040 | tf_op jit(solution)/shard_map/layer/pallas_call | solution.py:1102
  193.7 3.6 %finish.1 = (bf16[256,1024]{1,0:T(8,128)(2,1)}, f32[256,1024]{1,0:T(8,128)}, f32[1024]{0:T(1024)}, f32[1024]{0:T(1024)}, f32[256,384]{1,0:T(8,128)}, /*index=5*/...) custom-call(bf16[256,1024]{1,0:T(8,128)(2,1)} %bitcast.9, ...), custom_call_target="tpu_custom_call" | custom-call | tf_op jit(solution)/shard_map/finish/pallas_call | solution.py:1161
where the time goes:
time: 198 us
  Pallas kernels  197 us (99%)
    pallas_call x1, Pallas kernels, layer(): pl.pallas_call(layer_kernel, out_shape=(S((256, 1024), BF), S((256, 1024)...  193 us

commit v1 on v0

--- a/solution.py
+++ b/solution.py
@@ -847,10 +847,6 @@
             total += dot_nn(ds, keys)
         dq[top : top + T] = total
 
-    gz[0].wait_recv()
-    x_r[zc] = (pack_sum(zc) + z_r[0].astype(F32)).astype(BF)
-    gz[2].start()
-
     gq[...] = jnp.zeros_like(gq)
     own_a, other_xa, other_za, own_b, other_zb, other_xb, diag_a, diag_b = blocks
     order = (diag_a, diag_b, other_za, other_xb, other_xa, other_zb, own_a, own_b)
@@ -905,6 +901,10 @@
 
     lax.fori_loop(0, 9, block_step, 0)
     gx_copy(zn).start()
+    gz[0].wait_recv()
+    x_r[zc] = (pack_sum(zc) + z_r[0].astype(F32)).astype(BF)
+    gz[2].start()
+
 
     def sum_step(i, _):
         @pl.when(i < 7)

time: 198 us -> 194 us (0.980)
  Pallas kernels: 197 us -> 192 us
    pallas_call x1, Pallas kernels: 193 us -> 188 us  [layer(): pl.pallas_call(layer_kernel, out_shape=(S((256, 1024), BF), S((256, 1024)...]
where the time goes in v1:
time: 194 us; the launch traced here: 193 us
  Pallas kernels  192 us (99%)
    pallas_call x1, Pallas kernels, layer(): pl.pallas_call(layer_kernel, out_shape=(S((256, 1024), BF), S((256, 1024)...  188 us

profile of v1, /device:TPU:4, one launch (start us, length us, event | category | flops | bytes accessed | tf_op | source)
XLA Modules:
  0.0 192.6 jit_solution(13248035899038081101)
XLA Ops:
  0.6 188.2 %layer.1 = (bf16[256,1024]{1,0:T(8,128)(2,1)}, f32[256,1024]{1,0:T(8,128)}, bf16[2,128,1024]{2,1,0:T(8,128)(2,1)}, bf16[3,2,256,128]{3,2,1,0:T(8,128)(2,1)}, f32...) custom-call(bf16[256,1024]{1,0:T(8,128)(2,1)} %bitcast.8, ...), custom_call_target="tpu_custom_call" | custom-call | flops 20000000000 | bytes 41943040 | tf_op jit(solution)/shard_map/layer/pallas_call | solution.py:1102
  188.8 3.6 %finish.1 = (bf16[256,1024]{1,0:T(8,128)(2,1)}, f32[256,1024]{1,0:T(8,128)}, f32[1024]{0:T(1024)}, f32[1024]{0:T(1024)}, f32[256,384]{1,0:T(8,128)}, /*index=5*/...) custom-call(bf16[256,1024]{1,0:T(8,128)(2,1)} %bitcast.9, ...), custom_call_target="tpu_custom_call" | custom-call | tf_op jit(solution)/shard_map/finish/pallas_call | solution.py:1161

commit v2 on v1

--- a/solution.py
+++ b/solution.py
@@ -822,12 +822,13 @@
 
     x_r[znc] = pack_sum(znc).astype(BF)
     gz[0].start()
-    gx_copy(zc).start()
 
     dk[...] = jnp.zeros_like(dk)
     dv[...] = jnp.zeros_like(dv)
     for i in range(8):
         do_copy(0, i).wait_recv()
+        if i == 7:
+            gx_copy(zc).start()
         top = i * T
         start = first_columns(lens, top, T)
         query = qkv_v[top : top + T, :128]

time: 194 us -> 198 us (1.021)
  Pallas kernels: 192 us -> 197 us
    pallas_call x1, Pallas kernels: 188 us -> 193 us  [layer(): pl.pallas_call(layer_kernel, out_shape=(S((256, 1024), BF), S((256, 1024)...]
where the time goes in v2:
time: 198 us
  Pallas kernels  197 us (99%)
    pallas_call x1, Pallas kernels, layer(): pl.pallas_call(layer_kernel, out_shape=(S((256, 1024), BF), S((256, 1024)...  193 us

profile of v2, /device:TPU:4, one launch (start us, length us, event | category | flops | bytes accessed | tf_op | source)
XLA Modules:
  0.0 197.7 jit_solution(89361566256298252)
XLA Ops:
  0.6 193.2 %layer.1 = (bf16[256,1024]{1,0:T(8,128)(2,1)}, f32[256,1024]{1,0:T(8,128)}, bf16[2,128,1024]{2,1,0:T(8,128)(2,1)}, bf16[3,2,256,128]{3,2,1,0:T(8,128)(2,1)}, f32...) custom-call(bf16[256,1024]{1,0:T(8,128)(2,1)} %bitcast.8, ...), custom_call_target="tpu_custom_call" | custom-call | flops 20000000000 | bytes 41943040 | tf_op jit(solution)/shard_map/layer/pallas_call | solution.py:1103
  193.9 3.6 %finish.1 = (bf16[256,1024]{1,0:T(8,128)(2,1)}, f32[256,1024]{1,0:T(8,128)}, f32[1024]{0:T(1024)}, f32[1024]{0:T(1024)}, f32[256,384]{1,0:T(8,128)}, /*index=5*/...) custom-call(bf16[256,1024]{1,0:T(8,128)(2,1)} %bitcast.9, ...), custom_call_target="tpu_custom_call" | custom-call | tf_op jit(solution)/shard_map/finish/pallas_call | solution.py:1162
